TPU v7x, 128 devices: a whole 4x4x4 slice. The times are simulated.
128 devices in a mesh: dp: 4 (over z), mp: 32 (over x, y, core).
Axes of the slice: x: 4, y: 4, z: 4, core: 2. Of those that a mesh axis runs over, the one named last changes fastest.
Arguments:
- tokens: bfloat16 [16384, 4096], P(('dp', 'mp')), may hold values from -6 to 6
- expert_ids: int32 [16384, 1], P(('dp', 'mp')), may hold values from 0 to 63; in each aligned block of 128 rows (0 to 127, 128 to 255, ...) at most 3 rows name the same one
- gate_probs: float32 [16384, 1], P(('dp', 'mp')), may hold values from 0.3 to 1
- gate_weight: bfloat16 [64, 4096, 1536], P('mp', None, 'dp'), may hold values from -0.09375 to 0.09375
- up_weight: bfloat16 [64, 4096, 1536], P('mp', None, 'dp'), may hold values from -0.09375 to 0.09375
- down_weight: bfloat16 [64, 1536, 4096], P('mp', 'dp'), may hold values from -0.15625 to 0.15625
- sign_offset: int32 [1], replicated, may hold values from 1 to 999999999
Outputs:
- out_plus: bfloat16 [16384, 4096], P(('dp', 'mp'))
- out_minus: bfloat16 [16384, 4096], P(('dp', 'mp'))
Inputs may be any that keep to these rules, and one draw needn't show every extreme that they name: `expert_ids`: within each aligned block of 128 tokens (the tokens of one device) no expert is named by more than 3 routes, a bound that some block reaches.
All inputs are finite; a program needn't handle non-finite values.
Results may differ from a plain program's by a relative error of at most 0.01.
Values may be sent and summed in bfloat16 or wider, within the bound.
A program may use at most 128 MiB of HBM per device.

v0:
```python
import jax
import jax.numpy as jnp
from jax import lax
from jax.sharding import PartitionSpec as P

FF = 1536
epsilon_step = 0.005


def mixing(number):
    number = number ^ lax.shift_right_logical(number, jnp.full_like(number, 16))
    number = number * 73244475
    number = number ^ lax.shift_right_logical(number, jnp.full_like(number, 16))
    number = number * 73244475
    return number ^ lax.shift_right_logical(number, jnp.full_like(number, 16))


def sign_noise(offset_mixed, position, matrix_tag):
    hashed = mixing(position * 3 + matrix_tag ^ offset_mixed)
    parity = lax.shift_right_logical(hashed, jnp.full_like(hashed, 9)) & 1
    return (parity * 2 - 1).astype(jnp.float32)


def perturb(weight, noise, direction):
    return (weight.astype(jnp.float32) + direction * epsilon_step * noise).astype(jnp.bfloat16)


def expert_rows(arrived, weight_sets):
    lead_shape = arrived.shape
    model_width = lead_shape[-1]
    per_expert = []
    for local_expert in range(lead_shape[2]):
        flat_rows = arrived[:, :, local_expert].reshape(-1, model_width)
        by_pass = []
        for gate_moved, up_moved, down_moved in weight_sets[local_expert]:
            gate_act = jnp.dot(flat_rows, gate_moved, preferred_element_type=jnp.float32)
            up_act = jnp.dot(flat_rows, up_moved, preferred_element_type=jnp.float32)
            hidden = (jax.nn.silu(gate_act) * up_act).astype(jnp.bfloat16)
            by_pass.append(
                jnp.dot(hidden, down_moved, preferred_element_type=jnp.float32).astype(jnp.bfloat16)
            )
        stacked = jnp.stack(by_pass, axis=1).reshape(
            lead_shape[0], lead_shape[1], lead_shape[3], len(by_pass), model_width
        )
        per_expert.append(stacked)
    return jnp.stack(per_expert, axis=2)


def shards(tokens, expert_ids, gate_probs, gate_weight, up_weight, down_weight, sign_offset):
    mp_count = lax.axis_size("mp")
    tok_rows, model_width = tokens.shape
    route_count = expert_ids.shape[1]
    local_count = gate_weight.shape[0]
    quarter = gate_weight.shape[2]
    expert_count = local_count * mp_count
    capacity = 3 * tok_rows * route_count // (2 * expert_count)
    offset_mixed = mixing(sign_offset[0] * 668265261 + 12345)
    expert_base = lax.axis_index("mp") * local_count
    hidden_base = lax.axis_index("dp") * quarter
    width_axis = lax.broadcasted_iota(jnp.int32, (model_width, quarter), 0)
    unit_axis = lax.broadcasted_iota(jnp.int32, (model_width, quarter), 1) + hidden_base
    plus_sets = []
    minus_sets = []
    for local_expert in range(local_count):
        expert_global = expert_base + local_expert
        gate_pos = (expert_global * model_width + width_axis) * FF + unit_axis
        down_pos = (expert_global * FF + unit_axis.T) * model_width + width_axis.T
        noise_gate = sign_noise(offset_mixed, gate_pos, 0)
        noise_up = sign_noise(offset_mixed, gate_pos, 1)
        noise_down = sign_noise(offset_mixed, down_pos, 2)
        for direction, target in ((1.0, plus_sets), (-1.0, minus_sets)):
            target.append(
                (
                    perturb(gate_weight[local_expert], noise_gate, direction),
                    perturb(up_weight[local_expert], noise_up, direction),
                    perturb(down_weight[local_expert], noise_down, direction),
                )
            )
    route_flat = expert_ids.reshape(-1)
    expert_axis = lax.broadcasted_iota(jnp.int32, (route_flat.shape[0], expert_count), 1)
    onehot = (route_flat[:, None] == expert_axis).astype(jnp.int32)
    earlier = jnp.cumsum(onehot, axis=0, dtype=jnp.int32) - onehot
    rank_in = jnp.sum(earlier * onehot, axis=1, dtype=jnp.int32)
    slot_of = (route_flat * capacity + rank_in).reshape(tok_rows, route_count)
    slot_axis = lax.broadcasted_iota(jnp.int32, (expert_count * capacity, tok_rows), 0)
    selector = (slot_axis == slot_of[:, 0][None, :]).astype(jnp.float32)
    outgoing = jnp.dot(
        selector.astype(jnp.bfloat16), tokens, preferred_element_type=jnp.float32
    ).astype(jnp.bfloat16)
    outgoing = outgoing.reshape(mp_count, local_count, capacity, model_width)
    grouped = lax.all_gather(outgoing[None], "dp", axis=0, tiled=True)
    arrived = lax.all_to_all(grouped, "mp", split_axis=1, concat_axis=1, tiled=True)

    def finish(weight_sets):
        partials = expert_rows(arrived, weight_sets)
        returned = lax.all_to_all(partials, "mp", split_axis=1, concat_axis=1, tiled=True)
        summed = lax.psum_scatter(
            returned.astype(jnp.float32).astype(jnp.bfloat16), "dp", scatter_dimension=0, tiled=True
        ).astype(jnp.float32)
        return summed[0].astype(jnp.bfloat16)

    def combine(result, pass_index):
        flat_out = result.reshape(expert_count * capacity, result.shape[3], model_width)[
            :, pass_index
        ]
        picked = (
            jnp.take(flat_out, slot_of.reshape(-1), axis=0)
            .reshape(tok_rows, route_count, model_width)
            .astype(jnp.float32)
        )
        return jnp.sum(gate_probs[:, :, None] * picked, axis=1).astype(jnp.bfloat16)

    plus_result = finish([[entry_set] for entry_set in plus_sets])
    minus_result = finish([[entry_set] for entry_set in minus_sets])
    return (combine(plus_result, 0), combine(minus_result, 0))


def solution(mesh):
    in_specs = (
        P(("dp", "mp"), None),
        P(("dp", "mp"), None),
        P(("dp", "mp"), None),
        P("mp", None, "dp"),
        P("mp", None, "dp"),
        P("mp", "dp", None),
        P(),
    )
    out_specs = (P(("dp", "mp"), None), P(("dp", "mp"), None))
    return jax.shard_map(shards, mesh=mesh, in_specs=in_specs, out_specs=out_specs, check_vma=False)
```

profile of v0, /device:TPU:1, one launch (start us, length us, event | category | flops | bytes accessed | tf_op | source)
XLA Modules:
  0.0 660.6 jit_solution(3425733113894375996)
XLA Ops:
  7.2 0.8 fusion.194
  8.0 0.2 reduce_window_sum.11
  8.2 0.8 select_reduce_fusion
  9.1 1.2 compare_and_fusion
  10.2 0.5 copy-done.4
  10.8 1.7 convolution_convert_fusion.4
  12.5 2.7 broadcast_in_dim_reshape.3
  15.2 2.3 copy.13
  17.6 69.3 %all-gather.2.cloned.1.call-done = bf16[4,32,2,3,4096]{4,1,3,2,0:T(8,128)(2,1)} async-done(((bf16[1,32,2,3,4096]{4,1,3,2,0:T(8,128)(2,1)}), bf16[4,32,2,3,4096]{4,1,3,2,0:T(8,128)(2,1)}) %all-gather.2.cloned.1.call-update) | async-done | bytes 6291472 | tf_op jit(solution)/shard_map/all_gather | solution.py:91
  86.8 10.3 %copy.14 = bf16[4,32,2,3,4096]{4,0,3,2,1:T(4,128)(2,1)} copy(bf16[4,32,2,3,4096]{4,1,3,2,0:T(8,128)(2,1)} %all-gather.2.cloned.1.call-done) | data formatting | bytes 12582912 | tf_op jit(solution)/shard_map/all_gather | solution.py:91
  97.1 7.6 %all-to-all-start = ((bf16[4,32,2,3,4096]{4,0,3,2,1:T(4,128)(2,1)}), bf16[4,32,2,3,4096]{4,0,3,2,1:T(4,128)(2,1)}, u32[]{:S(2)}, u32[]{:S(2)}) async-start(bf16[4,32,2,3,4096]{4,0,3,2,1:T(4,128)(2,1)} %copy.14), calls=%async_computation | async-start | bytes 12582912 | tf_op jit(solution)/shard_map/all_to_all | solution.py:92
  104.7 0.2 reduce-scatter.3.cloned.1.call-start
  105.7 77.0 %all-to-all-done = bf16[4,32,2,3,4096]{4,0,3,2,1:T(4,128)(2,1)} async-done(((bf16[4,32,2,3,4096]{4,0,3,2,1:T(4,128)(2,1)}), bf16[4,32,2,3,4096]{4,0,3,2,1:T(4,128)(2,1)}, u32[]{:S(2)}, u32[]{:S(2)}) %all-to-all-start) | async-done | bytes 6291488 | tf_op jit(solution)/shard_map/all_to_all | solution.py:92
  182.7 6.9 %fusion.296 = (bf16[4,32,1,3,4096]{4,0,3,2,1:T(4,128)(2,1)}, bf16[4,32,1,3,4096]{4,0,3,2,1:T(4,128)(2,1)S(1)}) fusion(bf16[4,32,2,3,4096]{4,0,3,2,1:T(4,128)(2,1)} %all-to-all-done), kind=kLoop, calls=%fused_computation.284 | loop fusion | bytes 12582912 | tf_op jit(solution)/shard_map/slice | solution.py:33
  189.6 4.6 copy.16
  194.3 7.4 %reshape_squeeze.9 = bf16[384,4096]{1,0:T(8,128)(2,1)} reshape(bf16[4,32,1,3,4096]{4,3,1,0,2:T(4,128)(2,1)} %copy.16) | data formatting | bytes 6291456 | tf_op jit(solution)/shard_map/reshape;squeeze | solution.py:33
  201.7 7.5 %fusion.118 = f32[384,384]{1,0:T(8,128)S(1)} fusion(bf16[384,4096]{1,0:T(8,128)(2,1)} %reshape_squeeze.9, s32[4096]{0:T(1024)S(1)} %add_multiply_fusion.2, s32[]{:T(128)S(6)} %xor.269, s32[384]{0:T(512)S(1)} %iota_add_fusion, bf16[2,4096,384]{2,1,0:T(8,128)(2,1)} %param.12), kind=kOutput, calls=%fused_computation.151 | convolution fusion | flops 1239416832 | bytes 6899204 | tf_op jit(solution)/shard_map/dot_general | solution.py:36
  209.2 15.7 %convolution_convert_fusion.2 = bf16[384,4096]{1,0:T(8,128)(2,1)} fusion(s32[384]{0:T(512)S(1)} %get-tuple-element.9, s32[]{:T(128)S(6)} %xor.269, bf16[2,384,4096]{2,1,0:T(8,128)(2,1)} %param.14, bf16[384,4096]{1,0:T(8,128)(2,1)} %reshape_squeeze.9, s32[4096]{0:T(1024)S(1)} %add_multiply_fusion.2, s32[384]{0:T(512)S(1)} %iota_add_fusion, ...), kind=kOutput, calls=%fused_computation.92 | convolution fusion | flops 2484436992 | bytes 13193216 | tf_op jit(solution)/shard_map/dot_general | solution.py:40
  224.9 7.1 %stack_reshape_stack.13 = bf16[4,32,1,3,1,4096]{5,3,1,0,4,2:T(4,128)(2,1)} reshape(bf16[384,4096]{1,0:T(8,128)(2,1)} %convolution_convert_fusion.2) | data formatting | bytes 6291456 | tf_op jit(solution)/shard_map/stack;reshape;stack | solution.py:46
  232.0 7.4 %copy.15 = bf16[4,32,1,3,4096]{4,3,1,0,2:T(4,128)(2,1)} copy(bf16[4,32,1,3,4096]{4,0,3,2,1:T(4,128)(2,1)} %get-tuple-element.5) | data formatting | bytes 6291456 | tf_op jit(solution)/shard_map/slice | solution.py:33
  239.4 7.4 %reshape_squeeze.8 = bf16[384,4096]{1,0:T(8,128)(2,1)} reshape(bf16[4,32,1,3,4096]{4,3,1,0,2:T(4,128)(2,1)} %copy.15) | data formatting | bytes 6291456 | tf_op jit(solution)/shard_map/reshape;squeeze | solution.py:33
  246.8 7.5 %fusion.110 = f32[384,384]{1,0:T(8,128)S(1)} fusion(bf16[384,4096]{1,0:T(8,128)(2,1)} %reshape_squeeze.8, s32[]{:T(128)S(6)} %xor.269, s32[384]{0:T(512)S(1)} %iota_add_fusion, s32[4096]{0:T(1024)S(1)} %add_multiply_fusion.3, bf16[2,4096,384]{2,1,0:T(8,128)(2,1)} %param.12), kind=kOutput, calls=%fused_computation.147 | convolution fusion | flops 1239416832 | bytes 6899204 | tf_op jit(solution)/shard_map/dot_general | solution.py:36
  254.3 15.5 %convolution_convert_fusion.3 = bf16[384,4096]{1,0:T(8,128)(2,1)} fusion(s32[]{:T(128)S(6)} %xor.269, s32[384]{0:T(512)S(1)} %get-tuple-element.10, bf16[2,384,4096]{2,1,0:T(8,128)(2,1)} %param.14, bf16[384,4096]{1,0:T(8,128)(2,1)} %reshape_squeeze.8, s32[384]{0:T(512)S(1)} %iota_add_fusion, s32[4096]{0:T(1024)S(1)} %add_multiply_fusion.3, ...), kind=kOutput, calls=%fused_computation.93 | convolution fusion | flops 2484436992 | bytes 13193216 | tf_op jit(solution)/shard_map/dot_general | solution.py:40
  269.8 7.1 %stack_reshape_stack.12 = bf16[4,32,1,3,1,4096]{5,3,1,0,4,2:T(4,128)(2,1)} reshape(bf16[384,4096]{1,0:T(8,128)(2,1)} %convolution_convert_fusion.3) | data formatting | bytes 6291456 | tf_op jit(solution)/shard_map/stack;reshape;stack | solution.py:46
  276.9 8.7 %pad_maximum_fusion = bf16[4,32,2,3,1,4096]{5,3,1,0,4,2:T(4,128)(2,1)} fusion(bf16[4,32,1,3,1,4096]{5,3,1,0,4,2:T(4,128)(2,1)} %stack_reshape_stack.13, bf16[4,32,1,3,1,4096]{5,3,1,0,4,2:T(4,128)(2,1)} %stack_reshape_stack.12), kind=kLoop, calls=%fused_computation.20 | loop fusion | flops 3145728 | bytes 12582912 | tf_op jit(solution)/shard_map/stack | solution.py:46
  285.6 21.7 %copy.17 = bf16[4,32,2,3,1,4096]{5,0,4,3,2,1:T(4,128)(2,1)} copy(bf16[4,32,2,3,1,4096]{5,3,1,0,4,2:T(4,128)(2,1)} %pad_maximum_fusion) | data formatting | bytes 12582912 | tf_op jit(solution)/shard_map/stack | solution.py:46
  307.3 87.6 %all_to_all.15 = bf16[4,32,2,3,1,4096]{5,0,4,3,2,1:T(4,128)(2,1)S(1)} all-to-all(bf16[4,32,2,3,1,4096]{5,0,4,3,2,1:T(4,128)(2,1)} %copy.17), channel_id=1, replica_groups=mesh['dp'=4,'mp'=32] {'mp'}, dimensions={1} | all-to-all | bytes 12582912 | tf_op jit(solution)/shard_map/all_to_all | solution.py:96
  394.9 6.1 copy.18
  401.1 0.0 reduce-scatter.5.cloned.1.call-start
  401.2 7.5 %fusion.120 = f32[384,384]{1,0:T(8,128)S(1)} fusion(bf16[384,4096]{1,0:T(8,128)(2,1)} %reshape_squeeze.9, s32[4096]{0:T(1024)S(1)} %add_multiply_fusion.2, s32[]{:T(128)S(6)} %xor.269, s32[384]{0:T(512)S(1)} %iota_add_fusion, bf16[2,4096,384]{2,1,0:T(8,128)(2,1)} %param.12), kind=kOutput, calls=%fused_computation.152 | convolution fusion | flops 1239416832 | bytes 6899204 | tf_op jit(solution)/shard_map/dot_general | solution.py:36
  408.7 15.5 %convolution_convert_fusion = bf16[384,4096]{1,0:T(8,128)(2,1)} fusion(s32[384]{0:T(512)S(1)} %get-tuple-element.9, s32[]{:T(128)S(6)} %xor.269, bf16[2,384,4096]{2,1,0:T(8,128)(2,1)} %param.14, bf16[384,4096]{1,0:T(8,128)(2,1)} %reshape_squeeze.9, s32[4096]{0:T(1024)S(1)} %add_multiply_fusion.2, s32[384]{0:T(512)S(1)} %iota_add_fusion, ...), kind=kOutput, calls=%fused_computation.90 | convolution fusion | flops 2484436992 | bytes 13193216 | tf_op jit(solution)/shard_map/dot_general | solution.py:40
  424.2 7.1 %stack_reshape_stack.15 = bf16[4,32,1,3,1,4096]{5,3,1,0,4,2:T(4,128)(2,1)} reshape(bf16[384,4096]{1,0:T(8,128)(2,1)} %convolution_convert_fusion) | data formatting | bytes 6291456 | tf_op jit(solution)/shard_map/stack;reshape;stack | solution.py:46
  431.3 7.6 %fusion.112 = f32[384,384]{1,0:T(8,128)S(1)} fusion(bf16[384,4096]{1,0:T(8,128)(2,1)} %reshape_squeeze.8, s32[]{:T(128)S(6)} %xor.269, s32[384]{0:T(512)S(1)} %iota_add_fusion, s32[4096]{0:T(1024)S(1)} %add_multiply_fusion.3, bf16[2,4096,384]{2,1,0:T(8,128)(2,1)} %param.12), kind=kOutput, calls=%fused_computation.148 | convolution fusion | flops 1239416832 | bytes 6899204 | tf_op jit(solution)/shard_map/dot_general | solution.py:36
  438.9 15.9 %convolution_convert_fusion.1 = bf16[384,4096]{1,0:T(8,128)(2,1)} fusion(s32[]{:T(128)S(6)} %xor.269, s32[384]{0:T(512)S(1)} %get-tuple-element.10, bf16[2,384,4096]{2,1,0:T(8,128)(2,1)} %param.14, bf16[384,4096]{1,0:T(8,128)(2,1)} %reshape_squeeze.8, s32[384]{0:T(512)S(1)} %iota_add_fusion, s32[4096]{0:T(1024)S(1)} %add_multiply_fusion.3, ...), kind=kOutput, calls=%fused_computation.91 | convolution fusion | flops 2484436992 | bytes 13193216 | tf_op jit(solution)/shard_map/dot_general | solution.py:40
  454.8 7.1 %stack_reshape_stack.14 = bf16[4,32,1,3,1,4096]{5,3,1,0,4,2:T(4,128)(2,1)} reshape(bf16[384,4096]{1,0:T(8,128)(2,1)} %convolution_convert_fusion.1) | data formatting | bytes 6291456 | tf_op jit(solution)/shard_map/stack;reshape;stack | solution.py:46
  461.9 8.8 %pad_maximum_fusion.1 = bf16[4,32,2,3,1,4096]{5,3,1,0,4,2:T(4,128)(2,1)} fusion(bf16[4,32,1,3,1,4096]{5,3,1,0,4,2:T(4,128)(2,1)} %stack_reshape_stack.15, bf16[4,32,1,3,1,4096]{5,3,1,0,4,2:T(4,128)(2,1)} %stack_reshape_stack.14), kind=kLoop, calls=%fused_computation.21 | loop fusion | flops 3145728 | bytes 12582912 | tf_op jit(solution)/shard_map/stack | solution.py:46
  470.6 21.3 %copy.20 = bf16[4,32,2,3,1,4096]{5,0,4,3,2,1:T(4,128)(2,1)} copy(bf16[4,32,2,3,1,4096]{5,3,1,0,4,2:T(4,128)(2,1)} %pad_maximum_fusion.1) | data formatting | bytes 12582912 | tf_op jit(solution)/shard_map/stack | solution.py:46
  492.0 78.0 %all_to_all.16 = bf16[4,32,2,3,1,4096]{5,0,4,3,2,1:T(4,128)(2,1)S(1)} all-to-all(bf16[4,32,2,3,1,4096]{5,0,4,3,2,1:T(4,128)(2,1)} %copy.20), channel_id=1, replica_groups=mesh['dp'=4,'mp'=32] {'mp'}, dimensions={1} | all-to-all | bytes 12582912 | tf_op jit(solution)/shard_map/all_to_all | solution.py:96
  569.9 6.1 copy.21
  576.1 0.6 copy-done.5
  576.7 4.1 copy.19
  580.8 3.3 convert_element_type.262
  584.1 53.3 %reduce-scatter.5.cloned.1.call-done = bf16[1,32,2,3,1,4096]{5,1,4,3,2,0:T(8,128)(2,1)} async-done(((bf16[4,32,2,3,1,4096]{5,1,4,3,2,0:T(8,128)(2,1)}), bf16[1,32,2,3,1,4096]{5,1,4,3,2,0:T(8,128)(2,1)}) %reduce-scatter.5.cloned.1.call-update) | async-done | bytes 1572880 | tf_op jit(solution)/shard_map/reduce_scatter | solution.py:97
  637.4 4.1 copy.22
  641.5 4.3 convert_element_type.279
  645.8 2.2 gather_fusion
  648.0 3.9 gather_fusion.1
  651.9 1.9 multiply_convert_fusion
  (23 shorter events, 0.2 us)
Async XLA Ops:
  7.2 3.6 copy-start
  7.2 79.6 %all-gather.2.cloned.1.call-start = ((), (), s32[]{:S(2)}) async-start(), calls=%async_computation.5 | async-start | bytes 7864320 | tf_op jit(solution)/shard_map/all_gather | solution.py:91
  10.2 0.5 copy-start.4
  97.1 85.6 %all-to-all-start = ((bf16[4,32,2,3,4096]{4,0,3,2,1:T(4,128)(2,1)}), bf16[4,32,2,3,4096]{4,0,3,2,1:T(4,128)(2,1)}, u32[]{:S(2)}, u32[]{:S(2)}) async-start(bf16[4,32,2,3,4096]{4,0,3,2,1:T(4,128)(2,1)} %copy.14), calls=%async_computation | async-start | bytes 12582912 | tf_op jit(solution)/shard_map/all_to_all | solution.py:92
  104.7 471.9 %reduce-scatter.3.cloned.1.call-start = ((), (), s32[]{:S(2)}) async-start(), calls=%async_computation.6 | async-start | bytes 7864320 | tf_op jit(solution)/shard_map/reduce_scatter | solution.py:97
  401.1 236.3 %reduce-scatter.5.cloned.1.call-start = ((), (), s32[]{:S(2)}) async-start(), calls=%async_computation.7 | async-start | bytes 7864320 | tf_op jit(solution)/shard_map/reduce_scatter | solution.py:97
  576.0 0.6 copy-start.5
  645.8 8.0 %copy-start.1 = (bf16[128,4096]{1,0:T(8,128)(2,1)S(1)}, bf16[128,4096]{1,0:T(8,128)(2,1)}, u32[]{:S(2)}) copy-start(bf16[128,4096]{1,0:T(8,128)(2,1)} %param.9) | copy-start | bytes 3145732
  648.0 3.9 copy-start.2
  648.0 3.9 copy-start.3
  648.0 3.9 copy-start.6
Sparse Core Ops, SparseCore 0:
  17.7 69.0 all-gather.1
  401.2 61.1 reduce-scatter.2
  576.2 61.2 reduce-scatter.4
where the time goes:
time: 668 us; the launch traced here: 661 us
  waiting for transfers between devices  200 us (30%)
  blocking collectives  166 us (25%)
  local copies, waits for them, and re-layouts  156 us (23%)
  matrix products  94.5 us (14%)
  other arithmetic  22.4 us (3%)
  between operations  14.8 us (2%)
  starting transfers between devices  7.92 us (1%)
    all_to_all x2, blocking collectives, finish(): lax.all_to_all(partials, 'mp', split_axis=1, concat_axis=1, tiled=True)  166 us
    all_to_all x1, waiting for transfers between devices, shards(): lax.all_to_all(grouped, 'mp', split_axis=1, concat_axis=1, tiled=True)  77 us
    another operation x6, local copies, waits for them, and re-layouts, expert_rows(): return jnp.stack(per_expert, axis=2)  71.4 us
    all_gather x1, waiting for transfers between devices, shards(): grouped = lax.all_gather(outgoing[None], 'dp', axis=0, tiled=True)  69.3 us
    dot_general x4, matrix products, expert_rows(): jnp.dot(hidden, down_moved, preferred_element_type=jnp.float32)  62.6 us
    reduce_scatter x2, waiting for transfers between devices, finish(): lax.psum_scatter(returned.astype(jnp.float32).astype(jnp.bfloat16), 'dp',...  53.4 us
    dot_general x4, matrix products, expert_rows(): jnp.dot(flat_rows, gate_moved, preferred_element_type=jnp.float32)  30.1 us
    slice x3, local copies, waits for them, and re-layouts, expert_rows(): flat_rows = arrived[:, :, local_expert].reshape(-1, model_width)  19 us
  transfers between devices with their start and end apart: 4, of which 3 were waited for; matrix products, arithmetic and copies ran while one was open for 16% of the time, Pallas kernels for 0%

commit v1 on v0

--- a/solution.py
+++ b/solution.py
@@ -93,7 +93,10 @@
 
     def finish(weight_sets):
         partials = expert_rows(arrived, weight_sets)
-        returned = lax.all_to_all(partials, "mp", split_axis=1, concat_axis=1, tiled=True)
+        returned = jnp.concatenate(
+            lax.all_to_all(jnp.stack(jnp.split(partials, lax.axis_size("mp"), axis=1)), "mp", 0, 0),
+            axis=1,
+        )
         summed = lax.psum_scatter(
             returned.astype(jnp.float32).astype(jnp.bfloat16), "dp", scatter_dimension=0, tiled=True
         ).astype(jnp.float32)

time: 668 us -> 676 us (1.012)
  blocking collectives: 166 us -> 87.9 us
  local copies, waits for them, and re-layouts: 156 us -> 232 us
  starting transfers between devices: 7.92 us -> 33.2 us
  other arithmetic: 22.4 us -> 5.04 us
    all_to_all x2 -> x1, blocking collectives: 166 us -> 87.9 us  [finish(): lax.all_to_all(jnp.stack(jnp.split(partials, lax.axis_size('mp'), axis=1)...]
    unnamed x14 -> x102, local copies, waits for them, and re-layouts: 1.15 us -> 67.9 us
    another operation x0 -> x4, local copies, waits for them, and re-layouts: none -> 46.2 us  [finish(): jnp.stack(jnp.split(partials, lax.axis_size('mp'), axis=1))]
    another operation x6, local copies, waits for them, and re-layouts: 71.4 us -> 34.1 us  [expert_rows(): return jnp.stack(per_expert, axis=2)]
    another operation x2 -> x0, other arithmetic: 17.5 us -> none  [expert_rows(): return jnp.stack(per_expert, axis=2)]
    reshape x0 -> x2, local copies, waits for them, and re-layouts: none -> 14.9 us  [finish(): jnp.concatenate(lax.all_to_all(jnp.stack(jnp.split(partials, lax.axis_siz...]
    all_to_all x0 -> x1, starting transfers between devices: none -> 13.7 us  [finish(): lax.all_to_all(jnp.stack(jnp.split(partials, lax.axis_size('mp'), axis=1)...]
    all_to_all x2 -> x0, local copies, waits for them, and re-layouts: 12.2 us -> none  [finish(): lax.all_to_all(partials, 'mp', split_axis=1, concat_axis=1, tiled=True)]
  transfers between devices with their start and end apart: 4 -> 5, of which waited for: 3 -> 4; matrix products, arithmetic and copies ran while one was open for 16% -> 18% of each run, Pallas kernels for 0% -> 0%
where the time goes in v1:
time: 676 us; the launch traced here: 668 us
  local copies, waits for them, and re-layouts  232 us (34%)
  waiting for transfers between devices  204 us (30%)
  matrix products  91.1 us (13%)
  blocking collectives  87.9 us (13%)
  starting transfers between devices  33.2 us (5%)
  between operations  15 us (2%)
    all_to_all x1, blocking collectives, finish(): lax.all_to_all(jnp.stack(jnp.split(partials, lax.axis_size('mp'), axis=1)...  87.9 us
    all_to_all x1, waiting for transfers between devices, shards(): lax.all_to_all(grouped, 'mp', split_axis=1, concat_axis=1, tiled=True)  76.7 us
    all_gather x1, waiting for transfers between devices, shards(): grouped = lax.all_gather(outgoing[None], 'dp', axis=0, tiled=True)  69.2 us
    unnamed x102, local copies, waits for them, and re-layouts  67.9 us
    dot_general x4, matrix products, expert_rows(): jnp.dot(hidden, down_moved, preferred_element_type=jnp.float32)  62.1 us
    reduce_scatter x2, waiting for transfers between devices, finish(): lax.psum_scatter(returned.astype(jnp.float32).astype(jnp.bfloat16), 'dp',...  53.2 us
    another operation x4, local copies, waits for them, and re-layouts, finish(): jnp.stack(jnp.split(partials, lax.axis_size('mp'), axis=1))  46.2 us
    another operation x6, local copies, waits for them, and re-layouts, expert_rows(): return jnp.stack(per_expert, axis=2)  34.1 us
  transfers between devices with their start and end apart: 5, of which 4 were waited for; matrix products, arithmetic and copies ran while one was open for 18% of the time, Pallas kernels for 0%

profile of v1, /device:TPU:1, one launch (start us, length us, event | category | flops | bytes accessed | tf_op | source)
XLA Modules:
  0.0 668.2 jit_solution(3650965405681382184)
XLA Ops:
  10.8 1.8 convolution_convert_fusion.4
  12.6 2.7 broadcast_in_dim_reshape.3
  15.4 2.3 copy.133
  17.7 69.2 %all-gather.2.cloned.1.call-done = bf16[4,32,2,3,4096]{4,1,3,2,0:T(8,128)(2,1)} async-done(((bf16[1,32,2,3,4096]{4,1,3,2,0:T(8,128)(2,1)}), bf16[4,32,2,3,4096]{4,1,3,2,0:T(8,128)(2,1)}) %all-gather.2.cloned.1.call-update) | async-done | bytes 6291472 | tf_op jit(solution)/shard_map/all_gather | solution.py:91
  86.9 10.2 %copy.134 = bf16[4,32,2,3,4096]{4,0,3,2,1:T(4,128)(2,1)} copy(bf16[4,32,2,3,4096]{4,1,3,2,0:T(8,128)(2,1)} %all-gather.2.cloned.1.call-done) | data formatting | bytes 12582912 | tf_op jit(solution)/shard_map/all_gather | solution.py:91
  97.2 19.0 %all-to-all-start = ((bf16[4,32,2,3,4096]{4,0,3,2,1:T(4,128)(2,1)}), bf16[4,32,2,3,4096]{4,0,3,2,1:T(4,128)(2,1)}, u32[]{:S(2)}, u32[]{:S(2)}) async-start(bf16[4,32,2,3,4096]{4,0,3,2,1:T(4,128)(2,1)} %copy.134), calls=%async_computation | async-start | bytes 12582912 | tf_op jit(solution)/shard_map/all_to_all | solution.py:92
  116.9 76.7 %all-to-all-done = bf16[4,32,2,3,4096]{4,0,3,2,1:T(4,128)(2,1)} async-done(((bf16[4,32,2,3,4096]{4,0,3,2,1:T(4,128)(2,1)}), bf16[4,32,2,3,4096]{4,0,3,2,1:T(4,128)(2,1)}, u32[]{:S(2)}, u32[]{:S(2)}) %all-to-all-start) | async-done | bytes 6291488 | tf_op jit(solution)/shard_map/all_to_all | solution.py:92
  193.6 7.0 %fusion.360 = (bf16[4,32,1,3,4096]{4,0,3,2,1:T(4,128)(2,1)S(1)}, bf16[4,32,1,3,4096]{4,0,3,2,1:T(4,128)(2,1)}) fusion(bf16[4,32,2,3,4096]{4,0,3,2,1:T(4,128)(2,1)} %all-to-all-done), kind=kLoop, calls=%fused_computation.414 | loop fusion | bytes 12582912 | tf_op jit(solution)/shard_map/slice | solution.py:33
  200.5 4.8 copy.136
  205.3 7.5 %reshape_squeeze.9 = bf16[384,4096]{1,0:T(8,128)(2,1)} reshape(bf16[4,32,1,3,4096]{4,3,1,0,2:T(4,128)(2,1)} %copy.136) | data formatting | bytes 6291456 | tf_op jit(solution)/shard_map/reshape;squeeze | solution.py:33
  212.9 8.5 %fusion.118 = f32[384,384]{1,0:T(8,128)} fusion(bf16[384,4096]{1,0:T(8,128)(2,1)} %reshape_squeeze.9, s32[4096]{0:T(1024)S(1)} %add_multiply_fusion.2, s32[]{:T(128)S(6)} %xor.269, s32[384]{0:T(512)S(1)} %iota_add_fusion, bf16[2,4096,384]{2,1,0:T(8,128)(2,1)} %param.12), kind=kOutput, calls=%fused_computation.149 | convolution fusion | flops 1239416832 | bytes 6899204 | tf_op jit(solution)/shard_map/dot_general | solution.py:36
  221.3 5.5 fusion.120
  226.9 4.8 copy.135
  231.7 7.7 %reshape_squeeze.8 = bf16[384,4096]{1,0:T(8,128)(2,1)} reshape(bf16[4,32,1,3,4096]{4,3,1,0,2:T(4,128)(2,1)} %copy.135) | data formatting | bytes 6291456 | tf_op jit(solution)/shard_map/reshape;squeeze | solution.py:33
  239.4 8.5 %fusion.110 = f32[384,384]{1,0:T(8,128)} fusion(bf16[384,4096]{1,0:T(8,128)(2,1)} %reshape_squeeze.8, s32[]{:T(128)S(6)} %xor.269, s32[384]{0:T(512)S(1)} %iota_add_fusion, s32[4096]{0:T(1024)S(1)} %add_multiply_fusion.3, bf16[2,4096,384]{2,1,0:T(8,128)(2,1)} %param.12), kind=kOutput, calls=%fused_computation.145 | convolution fusion | flops 1239416832 | bytes 6899204 | tf_op jit(solution)/shard_map/dot_general | solution.py:36
  247.9 4.8 fusion.112
  252.7 16.0 %convolution_convert_fusion.2 = bf16[384,4096]{1,0:T(8,128)(2,1)} fusion(s32[384]{0:T(512)S(1)} %get-tuple-element.9, s32[]{:T(128)S(6)} %xor.269, bf16[2,384,4096]{2,1,0:T(8,128)(2,1)} %param.14, bf16[384,4096]{1,0:T(8,128)(2,1)} %reshape_squeeze.9, s32[4096]{0:T(1024)S(1)} %add_multiply_fusion.2, s32[384]{0:T(512)S(1)} %iota_add_fusion, ...), kind=kOutput, calls=%fused_computation.90 | convolution fusion | flops 2484436992 | bytes 13193216 | tf_op jit(solution)/shard_map/dot_general | solution.py:40
  268.7 7.4 %stack_reshape_stack.13 = bf16[4,32,1,3,1,4096]{5,3,1,0,4,2:T(4,128)(2,1)} reshape(bf16[384,4096]{1,0:T(8,128)(2,1)} %convolution_convert_fusion.2) | data formatting | bytes 6291456 | tf_op jit(solution)/shard_map/stack;reshape;stack | solution.py:46
  276.1 15.3 %convolution_convert_fusion.3 = bf16[384,4096]{1,0:T(8,128)(2,1)} fusion(s32[]{:T(128)S(6)} %xor.269, s32[384]{0:T(512)S(1)} %get-tuple-element.10, bf16[2,384,4096]{2,1,0:T(8,128)(2,1)} %param.14, bf16[384,4096]{1,0:T(8,128)(2,1)} %reshape_squeeze.8, s32[384]{0:T(512)S(1)} %iota_add_fusion, s32[4096]{0:T(1024)S(1)} %add_multiply_fusion.3, ...), kind=kOutput, calls=%fused_computation.91 | convolution fusion | flops 2484436992 | bytes 13193216 | tf_op jit(solution)/shard_map/dot_general | solution.py:40
  291.4 7.3 %stack_reshape_stack.12 = bf16[4,32,1,3,1,4096]{5,3,1,0,4,2:T(4,128)(2,1)} reshape(bf16[384,4096]{1,0:T(8,128)(2,1)} %convolution_convert_fusion.3) | data formatting | bytes 6291456 | tf_op jit(solution)/shard_map/stack;reshape;stack | solution.py:46
  298.8 4.3 constant_dynamic-update-slice_fusion.1
  303.1 2.3 constant_dynamic-update-slice_fusion
  331.4 21.6 %copy.168 = bf16[32,4,1,2,3,1,4096]{6,1,5,4,3,2,0:T(4,128)(2,1)} copy(bf16[32,4,1,2,3,1,4096]{6,4,1,3,5,2,0:T(4,128)(2,1)} %fusion.226) | data formatting | bytes 12582912 | tf_op jit(solution)/shard_map/stack | solution.py:97
  353.0 13.7 %all-to-all-start.1 = ((bf16[32,4,1,2,3,1,4096]{6,1,5,4,3,2,0:T(4,128)(2,1)}), bf16[32,4,1,2,3,1,4096]{6,1,5,4,3,2,0:T(4,128)(2,1)}, u32[]{:S(2)}, u32[]{:S(2)}) async-start(bf16[32,4,1,2,3,1,4096]{6,1,5,4,3,2,0:T(4,128)(2,1)} %copy.168), calls=%async_computation.1 | async-start | bytes 12582912 | tf_op jit(solution)/shard_map/all_to_all | solution.py:97
  366.9 15.4 %convolution_convert_fusion = bf16[384,4096]{1,0:T(8,128)(2,1)} fusion(s32[384]{0:T(512)S(1)} %get-tuple-element.9, s32[]{:T(128)S(6)} %xor.269, bf16[2,384,4096]{2,1,0:T(8,128)(2,1)} %param.14, bf16[384,4096]{1,0:T(8,128)(2,1)} %reshape_squeeze.9, s32[4096]{0:T(1024)S(1)} %add_multiply_fusion.2, s32[384]{0:T(512)S(1)} %iota_add_fusion, ...), kind=kOutput, calls=%fused_computation.88 | convolution fusion | flops 2484436992 | bytes 13193216 | tf_op jit(solution)/shard_map/dot_general | solution.py:40
  382.4 7.4 %stack_reshape_stack.15 = bf16[4,32,1,3,1,4096]{5,3,1,0,4,2:T(4,128)(2,1)} reshape(bf16[384,4096]{1,0:T(8,128)(2,1)} %convolution_convert_fusion) | data formatting | bytes 6291456 | tf_op jit(solution)/shard_map/stack;reshape;stack | solution.py:46
  389.7 15.3 %convolution_convert_fusion.1 = bf16[384,4096]{1,0:T(8,128)(2,1)} fusion(s32[]{:T(128)S(6)} %xor.269, s32[384]{0:T(512)S(1)} %get-tuple-element.10, bf16[2,384,4096]{2,1,0:T(8,128)(2,1)} %param.14, bf16[384,4096]{1,0:T(8,128)(2,1)} %reshape_squeeze.8, s32[384]{0:T(512)S(1)} %iota_add_fusion, s32[4096]{0:T(1024)S(1)} %add_multiply_fusion.3, ...), kind=kOutput, calls=%fused_computation.89 | convolution fusion | flops 2484436992 | bytes 13193216 | tf_op jit(solution)/shard_map/dot_general | solution.py:40
  405.0 7.5 %stack_reshape_stack.14 = bf16[4,32,1,3,1,4096]{5,3,1,0,4,2:T(4,128)(2,1)} reshape(bf16[384,4096]{1,0:T(8,128)(2,1)} %convolution_convert_fusion.1) | data formatting | bytes 6291456 | tf_op jit(solution)/shard_map/stack;reshape;stack | solution.py:46
  412.6 4.3 constant_dynamic-update-slice_fusion.3
  416.9 2.3 constant_dynamic-update-slice_fusion.2
  439.8 4.9 all-to-all-done.1
  444.7 8.9 %copy.169 = bf16[4,32,2,3,1,4096]{5,1,4,3,2,0:T(8,128)(2,1)} copy(bf16[4,32,2,3,1,4096]{5,0,3,2,1,4:T(4,128)(2,1)} %bitcast.42) | data formatting | bytes 12582912 | tf_op jit(solution)/shard_map/reshape | solution.py:96
  455.5 1.8 fusion.200
  457.3 1.8 fusion.199
  462.5 1.8 fusion.196
  464.3 1.8 fusion.195
  466.0 1.8 fusion.194
  467.8 22.0 %copy.202 = bf16[32,4,1,2,3,1,4096]{6,1,5,4,3,2,0:T(4,128)(2,1)} copy(bf16[32,4,1,2,3,1,4096]{6,4,1,3,5,2,0:T(4,128)(2,1)} %fusion.194) | data formatting | bytes 12582912 | tf_op jit(solution)/shard_map/stack | solution.py:97
  489.8 87.9 %all_to_all.15 = bf16[32,4,1,2,3,1,4096]{6,1,5,4,3,2,0:T(4,128)(2,1)S(1)} all-to-all(bf16[32,4,1,2,3,1,4096]{6,1,5,4,3,2,0:T(4,128)(2,1)} %copy.202), channel_id=1, replica_groups=mesh['dp'=4,'mp'=32] {'mp'}, dimensions={0} | all-to-all | bytes 12582912 | tf_op jit(solution)/shard_map/all_to_all | solution.py:97
  577.7 6.1 copy.203
  584.4 4.2 copy.170
  588.6 3.3 convert_element_type.262
  591.9 53.2 %reduce-scatter.5.cloned.1.call-done = bf16[1,32,2,3,1,4096]{5,1,4,3,2,0:T(8,128)(2,1)} async-done(((bf16[4,32,2,3,1,4096]{5,1,4,3,2,0:T(8,128)(2,1)}), bf16[1,32,2,3,1,4096]{5,1,4,3,2,0:T(8,128)(2,1)}) %reduce-scatter.5.cloned.1.call-update) | async-done | bytes 1572880 | tf_op jit(solution)/shard_map/reduce_scatter | solution.py:100
  645.0 4.1 copy.204
  649.1 4.3 convert_element_type.279
  653.4 2.2 gather_fusion
  655.6 3.9 gather_fusion.1
  659.5 1.9 multiply_convert_fusion
  (116 shorter events, 56.6 us)
Async XLA Ops:
  7.2 3.7 copy-start
  7.2 79.7 %all-gather.2.cloned.1.call-start = ((), (), s32[]{:S(2)}) async-start(), calls=%async_computation.5 | async-start | bytes 7864320 | tf_op jit(solution)/shard_map/all_gather | solution.py:91
  10.3 0.5 copy-start.10
  97.2 96.4 %all-to-all-start = ((bf16[4,32,2,3,4096]{4,0,3,2,1:T(4,128)(2,1)}), bf16[4,32,2,3,4096]{4,0,3,2,1:T(4,128)(2,1)}, u32[]{:S(2)}, u32[]{:S(2)}) async-start(bf16[4,32,2,3,4096]{4,0,3,2,1:T(4,128)(2,1)} %copy.134), calls=%async_computation | async-start | bytes 12582912 | tf_op jit(solution)/shard_map/all_to_all | solution.py:92
  205.3 16.0 %slice-start = ((s8[6291456]{0:T(1024)(128)(4,1)}), s8[2097152]{0:T(1024)(128)(4,1)S(1)}, s32[]{:S(2)}) async-start(s8[6291456]{0:T(1024)(128)(4,1)} %bitcast.480), calls=%async_computation.8 | async-start | bytes 4194304
  212.8 8.5 %copy-start.8 = (bf16[384,4096]{1,0:T(8,128)(2,1)S(1)}, bf16[384,4096]{1,0:T(8,128)(2,1)}, u32[]{:S(2)}) copy-start(bf16[384,4096]{1,0:T(8,128)(2,1)} %reshape_squeeze.9) | copy-start | bytes 9437188
  212.8 8.5 %slice-start.1 = ((s8[6291456]{0:T(1024)(128)(4,1)}), s8[4194304]{0:T(1024)(128)(4,1)S(1)}, s32[]{:S(2)}) async-start(s8[6291456]{0:T(1024)(128)(4,1)} %bitcast.480), calls=%async_computation.9 | async-start | bytes 8388608
  221.3 5.5 copy-start.5
  231.7 16.2 %slice-start.2 = ((s8[6291456]{0:T(1024)(128)(4,1)}), s8[2097152]{0:T(1024)(128)(4,1)S(1)}, s32[]{:S(2)}) async-start(s8[6291456]{0:T(1024)(128)(4,1)} %bitcast.482), calls=%async_computation.10 | async-start | bytes 4194304
  239.4 8.5 %copy-start.7 = (bf16[384,4096]{1,0:T(8,128)(2,1)S(1)}, bf16[384,4096]{1,0:T(8,128)(2,1)}, u32[]{:S(2)}) copy-start(bf16[384,4096]{1,0:T(8,128)(2,1)} %reshape_squeeze.8) | copy-start | bytes 9437188
  239.4 8.5 %slice-start.3 = ((s8[6291456]{0:T(1024)(128)(4,1)}), s8[4194304]{0:T(1024)(128)(4,1)S(1)}, s32[]{:S(2)}) async-start(s8[6291456]{0:T(1024)(128)(4,1)} %bitcast.482), calls=%async_computation.11 | async-start | bytes 8388608
  268.7 7.4 %copy-start.14 = (f32[384,384]{1,0:T(8,128)S(1)}, f32[384,384]{1,0:T(8,128)}, u32[]{:S(2)}) copy-start(f32[384,384]{1,0:T(8,128)} %fusion.110) | copy-start | bytes 1769476
  298.7 4.3 copy-start.4
  353.0 13.9 %copy-start.13 = (f32[384,384]{1,0:T(8,128)S(1)}, f32[384,384]{1,0:T(8,128)}, u32[]{:S(2)}) copy-start(f32[384,384]{1,0:T(8,128)} %fusion.120) | copy-start | bytes 1769476
  353.0 91.6 %all-to-all-start.1 = ((bf16[32,4,1,2,3,1,4096]{6,1,5,4,3,2,0:T(4,128)(2,1)}), bf16[32,4,1,2,3,1,4096]{6,1,5,4,3,2,0:T(4,128)(2,1)}, u32[]{:S(2)}, u32[]{:S(2)}) async-start(bf16[32,4,1,2,3,1,4096]{6,1,5,4,3,2,0:T(4,128)(2,1)} %copy.168), calls=%async_computation.1 | async-start | bytes 12582912 | tf_op jit(solution)/shard_map/all_to_all | solution.py:97
  366.7 217.7 %reduce-scatter.3.cloned.1.call-start = ((), (), s32[]{:S(2)}) async-start(), calls=%async_computation.6 | async-start | bytes 7864320 | tf_op jit(solution)/shard_map/reduce_scatter | solution.py:100
  412.6 4.3 copy-start.3
  419.2 19.8 %copy-start.2 = (bf16[4,32,2,3,1,4096]{5,3,1,0,4,2:T(4,128)(2,1)}, bf16[4,32,2,3,1,4096]{5,3,1,0,4,2:T(4,128)(2,1)S(1)}, u32[]{:S(2)}) copy-start(bf16[4,32,2,3,1,4096]{5,3,1,0,4,2:T(4,128)(2,1)S(1)} %constant_dynamic-update-slice_fusion.2) | copy-start | bytes 18874372
  453.5 191.5 %reduce-scatter.5.cloned.1.call-start = ((), (), s32[]{:S(2)}) async-start(), calls=%async_computation.7 | async-start | bytes 7864320 | tf_op jit(solution)/shard_map/reduce_scatter | solution.py:100
  583.7 0.6 copy-start.11
  653.4 8.0 %copy-start.1 = (bf16[128,4096]{1,0:T(8,128)(2,1)S(1)}, bf16[128,4096]{1,0:T(8,128)(2,1)}, u32[]{:S(2)}) copy-start(bf16[128,4096]{1,0:T(8,128)(2,1)} %param.9) | copy-start | bytes 3145732
  655.6 3.9 copy-start.6
  655.6 3.9 copy-start.9
  655.6 3.9 copy-start.12
Sparse Core Ops, SparseCore 0:
  17.8 69.0 all-gather.1
  453.7 72.2 reduce-scatter.2
  583.9 61.0 reduce-scatter.4
